TPU v7x, 32 devices: a whole 2x2x4 slice. The times are simulated.
32 devices in a mesh: shard: 16 (over z, y, x), ctx: 2 (over core).
Axes of the slice: x: 2, y: 2, z: 4, core: 2. Of those that a mesh axis runs over, the one named last changes fastest.
Arguments:
- tokens: bfloat16 [16, 2048, 384], P('shard', 'ctx'), may hold values from -6 to 6
- condition: bfloat16 [16, 384], P('shard'), may hold values from -6 to 6
- cotangent: bfloat16 [16, 2048, 384], P('shard', 'ctx'), may hold values from -6 to 6
- modulate_weight: float32 [384, 2304], P(None, 'shard'), may hold values from -0.3125 to 0.3125
- attend_weight: float32 [384, 1152], P(None, 'shard'), may hold values from -0.3125 to 0.3125
- project_weight: float32 [384, 384], P(None, 'shard'), may hold values from -0.875 to 0.875
- expand_weight: float32 [384, 1536], P(None, 'shard'), may hold values from -0.3125 to 0.3125
- reduce_weight: float32 [384, 1536], P(None, 'shard'), may hold values from -0.15625 to 0.15625
- bias_flat: float32 [5376], P('shard'), may hold values from -4 to 4
- modulate_moment: float32 [384, 2304], P(None, 'shard'), may hold values from -22 to 22, as said below
- attend_moment: float32 [384, 1152], P(None, 'shard'), may hold values from -22 to 22, as said below
- project_moment: float32 [384, 384], P(None, 'shard'), may hold values from -22 to 22, as said below
- expand_moment: float32 [384, 1536], P(None, 'shard'), may hold values from -22 to 22, as said below
- reduce_moment: float32 [384, 1536], P(None, 'shard'), may hold values from -22 to 22, as said below
- bias_moment: float32 [5376], P('shard'), may hold values from -4 to 4
Outputs:
- block_out: bfloat16 [16, 2048, 384], P('shard', 'ctx')
- tokens_grad: float32 [16, 2048, 384], P('shard', 'ctx')
- condition_grad: float32 [16, 384], P('shard')
- modulate_grad: float32 [384, 2304], P(None, 'shard')
- modulate_master: float32 [384, 2304], P(None, 'shard')
- modulate_momentum: float32 [384, 2304], P(None, 'shard')
- attend_grad: float32 [384, 1152], P(None, 'shard')
- attend_master: float32 [384, 1152], P(None, 'shard')
- attend_momentum: float32 [384, 1152], P(None, 'shard')
- project_grad: float32 [384, 384], P(None, 'shard')
- project_master: float32 [384, 384], P(None, 'shard')
- project_momentum: float32 [384, 384], P(None, 'shard')
- expand_grad: float32 [384, 1536], P(None, 'shard')
- expand_master: float32 [384, 1536], P(None, 'shard')
- expand_momentum: float32 [384, 1536], P(None, 'shard')
- reduce_grad: float32 [384, 1536], P(None, 'shard')
- reduce_master: float32 [384, 1536], P(None, 'shard')
- reduce_momentum: float32 [384, 1536], P(None, 'shard')
- bias_grad: float32 [5376], P('shard')
- bias_master: float32 [5376], P('shard')
- bias_momentum: float32 [5376], P('shard')
Inputs may be any that keep to these rules, and one draw needn't show every extreme that they name: `modulate_moment`: entries of the old momentum. `attend_moment`: entries of the old momentum. `project_moment`: entries of the old momentum. `expand_moment`: entries of the old momentum. `reduce_moment`: entries of the old momentum.
All inputs are finite; a program needn't handle non-finite values.
Results may differ from a plain program's by a relative error of at most 0.011.
The roundings to bfloat16 on the way count: a program that leaves them out, or rounds other values in their place, can miss the bound.
Values may be sent and summed in bfloat16 or wider, within the bound.
A program may use at most 320 MiB of HBM per device.

v0:
```python
import math
import jax
import jax.numpy as jnp
from jax import lax
from jax.sharding import PartitionSpec as P

D = 384
FF = 1536
HEADS = 6
HEAD_DIM = 64
SEQ = 2048
NS_ITERS = 5
norm_eps = 1e-06
newton_a = 3.4445
newton_b = -4.775
newton_c = 2.0315
moment_decay = 0.95
matrix_rate = 0.5
bias_rate = 0.1
precise = lax.Precision.HIGHEST


def silu_of(values):
    return values * jax.nn.sigmoid(values)


def gelu_tanh(values):
    return (
        0.5
        * values
        * (1.0 + jnp.tanh(0.7978845608028654 * (values + 0.044715 * values * values * values)))
    )


def normalize(values):
    centered = values - jnp.mean(values, axis=-1, keepdims=True)
    inverse = lax.rsqrt(jnp.mean(centered * centered, axis=-1, keepdims=True) + norm_eps)
    return (centered * inverse, inverse)


def norm_back(grad_normed, normed, inverse):
    first = jnp.mean(grad_normed, axis=-1, keepdims=True)
    second = jnp.mean(grad_normed * normed, axis=-1, keepdims=True)
    return (grad_normed - first - normed * second) * inverse


def contract_rows(left, right):
    return lax.dot_general(
        left, right, (((0,), (0,)), ((), ())), preferred_element_type=jnp.float32
    )


def contract_cols(left, right):
    return lax.dot_general(
        left, right, (((1,), (1,)), ((), ())), preferred_element_type=jnp.float32
    )


def split_heads(array):
    return array.reshape(array.shape[0], array.shape[1], HEADS, HEAD_DIM)


def newton_whole(matrix):
    norm_value = jnp.sqrt(jnp.sum(matrix * matrix))
    iterate = matrix / (norm_value + 1e-07)
    for sweep_index in range(NS_ITERS):
        gram_now = jnp.dot(iterate, iterate.T, precision=precise)
        polynomial = newton_b * gram_now + newton_c * jnp.dot(gram_now, gram_now, precision=precise)
        iterate = newton_a * iterate + jnp.dot(polynomial, iterate, precision=precise)
    return iterate


def on_device(
    tokens,
    condition,
    cotangent,
    modulate_weight,
    attend_weight,
    project_weight,
    expand_weight,
    reduce_weight,
    bias_flat,
    modulate_moment,
    attend_moment,
    project_moment,
    expand_moment,
    reduce_moment,
    bias_moment,
):
    lat_local, seq_local = (tokens.shape[0], tokens.shape[1])
    row_count = lat_local * seq_local
    bfloat = jnp.bfloat16
    single = jnp.float32
    full_params = (
        lax.all_gather(modulate_weight.astype(bfloat), "shard", axis=1, tiled=True),
        lax.all_gather(attend_weight.astype(bfloat), "shard", axis=1, tiled=True),
        lax.all_gather(project_weight.astype(bfloat), "shard", axis=1, tiled=True),
        lax.all_gather(expand_weight.astype(bfloat), "shard", axis=1, tiled=True),
        lax.all_gather(reduce_weight.astype(bfloat), "shard", axis=1, tiled=True),
        lax.all_gather(bias_flat.astype(bfloat), "shard", axis=0, tiled=True),
    )
    modulate_full, attend_full, project_full, expand_full, reduce_full, bias_low = full_params
    bias_full = bias_low.astype(single)
    bias_mod = bias_full[: 6 * D]
    bias_query = bias_full[6 * D : 7 * D]
    bias_value = bias_full[7 * D : 8 * D]
    bias_proj = bias_full[8 * D : 9 * D]
    bias_expand = bias_full[9 * D : 9 * D + FF]
    bias_reduce = bias_full[9 * D + FF :]
    cond_float = condition.astype(single)
    silu_low = silu_of(cond_float).astype(bfloat)
    modulation = jnp.dot(silu_low, modulate_full, preferred_element_type=single) + bias_mod
    shift_one, scale_one, gate_one, shift_two, scale_two, gate_two = jnp.split(
        modulation[:, None, :], 6, axis=-1
    )
    tok_float = tokens.astype(single)
    normed_one, inverse_one = normalize(tok_float)
    attend_in = (normed_one * (1.0 + scale_one) + shift_one).astype(bfloat).reshape(row_count, D)
    qkv_bias = jnp.concatenate([bias_query, jnp.zeros((D,), single), bias_value])
    qkv_low = (
        (jnp.dot(attend_in, attend_full, preferred_element_type=single) + qkv_bias)
        .astype(bfloat)
        .reshape(lat_local, seq_local, 3 * D)
    )
    queries = qkv_low[:, :, :D]
    keys_all, values_all = (
        lax.all_gather(qkv_low[:, :, D : 2 * D], "ctx", axis=1, tiled=True),
        lax.all_gather(qkv_low[:, :, 2 * D :], "ctx", axis=1, tiled=True),
    )
    score_scale = HEAD_DIM ** (-0.5)
    query_heads = split_heads(queries)
    key_heads = split_heads(keys_all)
    value_heads = split_heads(values_all)
    scores = (
        jnp.einsum("lqhd,lkhd->lhqk", query_heads, key_heads, preferred_element_type=single)
        * score_scale
    )
    row_max = jnp.max(scores, axis=-1, keepdims=True)
    shifted = jnp.exp(scores - row_max)
    row_total = jnp.sum(shifted, axis=-1, keepdims=True)
    attn_probs = shifted / row_total
    log_total = row_max + jnp.log(row_total)
    context = (
        jnp.einsum(
            "lhqk,lkhd->lqhd", attn_probs.astype(bfloat), value_heads, preferred_element_type=single
        )
        .astype(bfloat)
        .reshape(row_count, D)
    )
    attended = (jnp.dot(context, project_full, preferred_element_type=single) + bias_proj).reshape(
        lat_local, seq_local, D
    )
    middle = tok_float + gate_one * attended
    normed_two, inverse_two = normalize(middle)
    expand_in = (normed_two * (1.0 + scale_two) + shift_two).astype(bfloat).reshape(row_count, D)
    hidden = jnp.dot(expand_in, expand_full, preferred_element_type=single) + bias_expand
    act_low = gelu_tanh(hidden).astype(bfloat)
    mlp_out = (contract_cols(act_low, reduce_full) + bias_reduce).reshape(lat_local, seq_local, D)
    block_out = (middle + gate_two * mlp_out).astype(bfloat)
    grad_out = cotangent.astype(single)
    grad_gate_two = jnp.sum(grad_out * mlp_out, axis=1)
    grad_mlp = (gate_two * grad_out).astype(bfloat).reshape(row_count, D)
    reduce_grad = contract_rows(grad_mlp, act_low)
    grad_act = jnp.dot(grad_mlp, reduce_full, preferred_element_type=single)
    grad_hidden = jax.vjp(gelu_tanh, hidden)[1](grad_act)[0].astype(bfloat)
    expand_grad = contract_rows(expand_in, grad_hidden)
    grad_in_two = contract_cols(grad_hidden, expand_full).reshape(lat_local, seq_local, D)
    grad_shift_two = jnp.sum(grad_in_two, axis=1)
    grad_scale_two = jnp.sum(grad_in_two * normed_two, axis=1)
    grad_middle = grad_out + norm_back(grad_in_two * (1.0 + scale_two), normed_two, inverse_two)
    grad_gate_one = jnp.sum(grad_middle * attended, axis=1)
    grad_attended = (gate_one * grad_middle).astype(bfloat).reshape(row_count, D)
    project_grad = contract_rows(context, grad_attended)
    grad_context = split_heads(
        contract_cols(grad_attended, project_full).astype(bfloat).reshape(lat_local, seq_local, D)
    )
    scores_again = (
        jnp.einsum("lqhd,lkhd->lhqk", query_heads, key_heads, preferred_element_type=single)
        * score_scale
    )
    probs_again = jnp.exp(scores_again - log_total)
    grad_probs = jnp.einsum(
        "lqhd,lkhd->lhqk", grad_context, value_heads, preferred_element_type=single
    )
    value_part = jnp.einsum(
        "lhqk,lqhd->lkhd", probs_again.astype(bfloat), grad_context, preferred_element_type=single
    )
    grad_scores = (
        probs_again * (grad_probs - jnp.sum(probs_again * grad_probs, axis=-1, keepdims=True))
    ).astype(bfloat)
    query_grad = (
        jnp.einsum("lhqk,lkhd->lqhd", grad_scores, key_heads, preferred_element_type=single)
        * score_scale
    )
    key_part = (
        jnp.einsum("lhqk,lqhd->lkhd", grad_scores, query_heads, preferred_element_type=single)
        * score_scale
    )
    seq_whole = key_part.shape[1]
    key_grad, value_grad = (
        lax.psum_scatter(
            key_part.reshape(lat_local, seq_whole, D), "ctx", scatter_dimension=1, tiled=True
        ),
        lax.psum_scatter(
            value_part.reshape(lat_local, seq_whole, D), "ctx", scatter_dimension=1, tiled=True
        ),
    )
    grad_qkv = (
        jnp.concatenate(
            [query_grad.reshape(lat_local, seq_local, D), key_grad, value_grad], axis=-1
        )
        .astype(bfloat)
        .reshape(row_count, 3 * D)
    )
    attend_grad = contract_rows(attend_in, grad_qkv)
    grad_in_one = contract_cols(grad_qkv, attend_full).reshape(lat_local, seq_local, D)
    grad_shift_one = jnp.sum(grad_in_one, axis=1)
    grad_scale_one = jnp.sum(grad_in_one * normed_one, axis=1)
    tokens_grad = grad_middle + norm_back(grad_in_one * (1.0 + scale_one), normed_one, inverse_one)
    grad_mod = jnp.concatenate(
        [
            grad_shift_one,
            grad_scale_one,
            grad_gate_one,
            grad_shift_two,
            grad_scale_two,
            grad_gate_two,
        ],
        axis=-1,
    )
    modulate_grad = lax.dot_general(
        silu_low.astype(single), grad_mod, (((0,), (0,)), ((), ())), precision=precise
    )
    grad_silu = lax.dot_general(
        grad_mod, modulate_full.astype(single), (((1,), (1,)), ((), ())), precision=precise
    )
    cond_part = jax.vjp(silu_of, cond_float)[1](grad_silu)[0]
    bias_grad = jnp.concatenate(
        [
            jnp.sum(grad_mod, axis=0),
            jnp.sum(grad_qkv[:, :D].astype(single), axis=0),
            jnp.sum(grad_qkv[:, 2 * D :].astype(single), axis=0),
            jnp.sum(grad_attended.astype(single), axis=0),
            jnp.sum(grad_hidden.astype(single), axis=0),
            jnp.sum(grad_mlp.astype(single), axis=0),
        ]
    )
    shard_sums = (
        lax.psum_scatter(modulate_grad, "shard", scatter_dimension=1, tiled=True),
        lax.psum_scatter(attend_grad, "shard", scatter_dimension=1, tiled=True),
        lax.psum_scatter(project_grad, "shard", scatter_dimension=1, tiled=True),
        lax.psum_scatter(expand_grad, "shard", scatter_dimension=1, tiled=True),
        lax.psum_scatter(reduce_grad, "shard", scatter_dimension=1, tiled=True),
        lax.psum_scatter(bias_grad, "shard", scatter_dimension=0, tiled=True),
    )
    ctx_sums = lax.psum(
        (
            shard_sums[0],
            shard_sums[1],
            shard_sums[2],
            shard_sums[3],
            shard_sums[4],
            shard_sums[5],
            cond_part,
        ),
        "ctx",
    )
    shard_count = lax.axis_size("shard")
    grad_scale = 1.0 / math.sqrt(lat_local * shard_count * SEQ)
    grads = tuple((summed * grad_scale for summed in ctx_sums[:6]))
    condition_grad = ctx_sums[6]
    old_moments = (
        modulate_moment,
        attend_moment,
        project_moment,
        expand_moment,
        reduce_moment,
        bias_moment,
    )
    new_moments = tuple(
        (moment_decay * old_moment + grad_item for old_moment, grad_item in zip(old_moments, grads))
    )
    matrices = new_moments[:5]
    whole = (
        lax.all_gather(matrices[0], "shard", axis=1, tiled=True),
        lax.all_gather(matrices[1], "shard", axis=1, tiled=True),
        lax.all_gather(matrices[2], "shard", axis=1, tiled=True),
        lax.all_gather(matrices[3], "shard", axis=1, tiled=True),
        lax.all_gather(matrices[4], "shard", axis=1, tiled=True),
    )
    position = lax.axis_index("shard")
    directions = tuple(
        (
            lax.dynamic_slice_in_dim(
                newton_whole(whole_matrix),
                position * local_matrix.shape[1],
                local_matrix.shape[1],
                1,
            )
            for whole_matrix, local_matrix in zip(whole, matrices)
        )
    )
    masters = (modulate_weight, attend_weight, project_weight, expand_weight, reduce_weight)
    new_masters = tuple(
        (
            master
            - matrix_rate * 0.2 * math.sqrt(max(D, master.shape[1] * shard_count)) * direction
            for master, direction in zip(masters, directions)
        )
    )
    new_bias = bias_flat - bias_rate * new_moments[5]
    return (
        block_out,
        tokens_grad,
        condition_grad,
        grads[0],
        new_masters[0],
        new_moments[0],
        grads[1],
        new_masters[1],
        new_moments[1],
        grads[2],
        new_masters[2],
        new_moments[2],
        grads[3],
        new_masters[3],
        new_moments[3],
        grads[4],
        new_masters[4],
        new_moments[4],
        grads[5],
        new_bias,
        new_moments[5],
    )


def solution(mesh):
    placed = (
        P("shard", "ctx", None),
        P("shard", None),
        P("shard", "ctx", None),
        P(None, "shard"),
        P(None, "shard"),
        P(None, "shard"),
        P(None, "shard"),
        P(None, "shard"),
        P("shard"),
        P(None, "shard"),
        P(None, "shard"),
        P(None, "shard"),
        P(None, "shard"),
        P(None, "shard"),
        P("shard"),
    )
    return jax.shard_map(
        on_device,
        mesh=mesh,
        in_specs=placed,
        out_specs=(
            P("shard", "ctx", None),
            P("shard", "ctx", None),
            P("shard", None),
            P(None, "shard"),
            P(None, "shard"),
            P(None, "shard"),
            P(None, "shard"),
            P(None, "shard"),
            P(None, "shard"),
            P(None, "shard"),
            P(None, "shard"),
            P(None, "shard"),
            P(None, "shard"),
            P(None, "shard"),
            P(None, "shard"),
            P(None, "shard"),
            P(None, "shard"),
            P(None, "shard"),
            P("shard"),
            P("shard"),
            P("shard"),
        ),
        check_vma=False,
    )
```

profile of v0, /device:TPU:0, one launch (start us, length us, event | category | flops | bytes accessed | tf_op | source)
XLA Modules:
  0.0 1508.2 jit_solution(14004670184364255658)
XLA Ops:
  11.9 78.7 %all-reduce = bf16[5376]{0:T(1024)(128)(2,1)S(1)} all-reduce(bf16[5376]{0:T(1024)(128)(2,1)S(1)} %dynamic-update-slice), channel_id=1, replica_groups=mesh['shard'=16,'ctx'=2] {'shard'}, use_global_device_ids=true, to_apply=%add | all-reduce | flops 5376 | bytes 21504
  94.5 41.3 %all_gather.41 = bf16[384,1152]{0,1:T(8,128)(2,1)S(1)} all-gather(bf16[384,72]{0,1:T(8,128)(2,1)S(1)} %convert_element_type.109), channel_id=1, replica_groups=mesh['shard'=16,'ctx'=2] {'shard'}, dimensions={1}, use_global_device_ids=true | all-gather | bytes 940032 | tf_op jit(solution)/shard_map/all_gather | solution.py:96
  144.2 38.3 %all_gather.44 = bf16[384,384]{0,1:T(8,128)(2,1)S(1)} all-gather(bf16[384,24]{0,1:T(8,128)(2,1)S(1)} %convert_element_type.115), channel_id=1, replica_groups=mesh['shard'=16,'ctx'=2] {'shard'}, dimensions={1}, use_global_device_ids=true | all-gather | bytes 313344 | tf_op jit(solution)/shard_map/all_gather | solution.py:97
  184.8 19.5 %multiply_reduce_fusion.1 = (f32[6,1024]{1,0:T(8,128)S(1)}, f32[6,1024,2048]{2,1,0:T(8,128)}) fusion(bf16[1024,6,64]{0,2,1:T(8,128)(2,1)S(1)} %bitcast.267, bf16[2048,6,64]{0,2,1:T(8,128)(2,1)S(1)} %bitcast.262), kind=kOutput, calls=%fused_computation.6 | convolution fusion | flops 1635772416 | bytes 52715520 | tf_op jit(solution)/shard_map/lqhd,lkhd->lhqk/dot_general | solution.py:135
  204.2 20.5 %fusion = f32[6,1024]{1,0:T(8,128)S(1)} fusion(f32[6,1024,2048]{2,1,0:T(8,128)} %get-tuple-element.163, f32[6,1024]{1,0:T(8,128)S(1)} %get-tuple-element.162), kind=kLoop, calls=%fused_computation.5 | loop fusion | flops 37742592 | bytes 50380800 | tf_op jit(solution)/shard_map/reduce_sum | solution.py:140
  226.5 19.8 %fusion.35 = bf16[6,64,1024]{2,1,0:T(8,128)(2,1)S(1)} fusion(bf16[2048,6,64]{0,2,1:T(8,128)(2,1)S(1)} %bitcast.271, f32[6,1024,2048]{2,1,0:T(8,128)} %get-tuple-element.163, f32[6,1024]{1,0:T(8,128)S(1)} %fusion, f32[6,1024]{1,0:T(8,128)S(1)} %get-tuple-element.162), kind=kOutput, calls=%fused_computation.93 | convolution fusion | flops 1661337600 | bytes 52740096 | tf_op jit(solution)/shard_map/lhqk,lkhd->lqhd/dot_general | solution.py:144
  248.7 7.0 multiply_convert_fusion.1
  255.7 24.9 %all-gather.18.cloned.1.call-done = bf16[384,1536]{0,1:T(8,128)(2,1)} async-done(((bf16[384,96]{0,1:T(8,128)(2,1)}), bf16[384,1536]{0,1:T(8,128)(2,1)}) %all-gather.18.cloned.1.call-update) | async-done | bytes 1179664 | tf_op jit(solution)/shard_map/all_gather | solution.py:99
  280.6 9.7 convert_reduce_fusion
  301.2 19.6 %fusion.2 = f32[6,64,2048]{2,1,0:T(8,128)} fusion(bf16[1024,6,64]{0,2,1:T(8,128)(2,1)S(1)} %bitcast.269, f32[6,1024,2048]{2,1,0:T(8,128)} %get-tuple-element.163, f32[6,1024]{1,0:T(8,128)S(1)} %log_add_fusion), kind=kOutput, calls=%fused_computation.8 | convolution fusion | flops 1648361472 | bytes 54288384 | tf_op jit(solution)/shard_map/lhqk,lqhd->lkhd/dot_general | solution.py:185
  320.9 35.1 %multiply_reduce_fusion = (f32[6,1024]{1,0:T(8,128)S(1)}, f32[6,1024,2048]{2,1,0:T(8,128)}) fusion(f32[6,1024,2048]{2,1,0:T(8,128)} %get-tuple-element.163, f32[6,1024]{1,0:T(8,128)S(1)} %log_add_fusion, bf16[1024,6,64]{0,2,1:T(8,128)(2,1)S(1)} %bitcast.270, bf16[2048,6,64]{0,2,1:T(8,128)(2,1)} %bitcast.272), kind=kOutput, calls=%fused_computation.1 | convolution fusion | flops 1660938240 | bytes 103071744 | tf_op jit(solution)/shard_map/lqhd,lkhd->lhqk/dot_general | solution.py:182
  356.0 40.5 %multiply_convert_fusion = bf16[6,1024,2048]{2,1,0:T(8,128)(2,1)} fusion(f32[6,1024,2048]{2,1,0:T(8,128)} %get-tuple-element.169, f32[6,1024,2048]{2,1,0:T(8,128)} %get-tuple-element.163, f32[6,1024]{1,0:T(8,128)S(1)} %get-tuple-element.168, f32[6,1024]{1,0:T(8,128)S(1)} %log_add_fusion), kind=kLoop, calls=%fused_computation | loop fusion | flops 62914560 | bytes 125878272 | tf_op jit(solution)/shard_map/convert_element_type | solution.py:190
  396.6 14.3 convolution_multiply_fusion
  412.3 13.9 multiply_convert_fusion.2
  442.1 5.1 fusion.70
  448.8 5.4 fusion.100
  458.6 115.5 %reduce-scatter.22.cloned.1.call-done = f32[144,384]{1,0:T(8,128)} async-done(((f32[2304,384]{1,0:T(8,128)}), f32[144,384]{1,0:T(8,128)}) %reduce-scatter.22.cloned.1.call-update) | async-done | bytes 221200
  576.0 130.6 %reduce-scatter.20.cloned.1.call-done = f32[384,96]{0,1:T(8,128)} async-done(((f32[384,1536]{0,1:T(8,128)}), f32[384,96]{0,1:T(8,128)}) %reduce-scatter.20.cloned.1.call-update) | async-done | bytes 147472 | tf_op jit(solution)/shard_map/reduce_scatter | solution.py:253
  706.6 132.9 %reduce-scatter.18.cloned.1.call-done = f32[384,96]{0,1:T(8,128)} async-done(((f32[384,1536]{0,1:T(8,128)}), f32[384,96]{0,1:T(8,128)}) %reduce-scatter.18.cloned.1.call-update) | async-done | bytes 147472 | tf_op jit(solution)/shard_map/reduce_scatter | solution.py:252
  839.5 130.6 %reduce-scatter.24.cloned.1.call-done = f32[384,72]{0,1:T(8,128)} async-done(((f32[384,1152]{0,1:T(8,128)}), f32[384,72]{0,1:T(8,128)}) %reduce-scatter.24.cloned.1.call-update) | async-done | bytes 110608
  971.8 19.1 %all-reduce.8.cloned.1.call-done = (f32[384,144]{1,0:T(8,128)}, f32[384,72]{0,1:T(8,128)}, f32[384,96]{0,1:T(8,128)}, f32[384,96]{0,1:T(8,128)}) async-done(((f32[384,144]{1,0:T(8,128)}, f32[384,72]{0,1:T(8,128)}, f32[384,96]{0,1:T(8,128)}, f32[384,96]{0,1:T(8,128)}), (f32[384,144]{1,0:T(8,128)}, f32[384,72]{0,1:T(8,128)}, f32[384,96]{0,1:T(8,128)}, f32[384,96]{0,1:T(8,128)})) %all-reduce.8.cloned.1.call-update) | async-done | bytes 626704 | tf_op jit(solution)/shard_map/psum | solution.py:256
  997.2 77.1 %all-reduce.3 = f32[5376]{0:T(1024)S(1)} all-reduce(f32[5376]{0:T(1024)S(1)} %constant_dynamic-update-slice_fusion.7), channel_id=9, replica_groups=mesh['shard'=16,'ctx'=2] {'shard'}, use_global_device_ids=true, to_apply=%region_40.0.clone | all-reduce | flops 5376 | bytes 43008
  1075.2 44.6 %reduce-scatter.26.cloned.1.call-done = f32[384,24]{0,1:T(8,128)} async-done(((f32[384,384]{0,1:T(8,128)}), f32[384,24]{0,1:T(8,128)}) %reduce-scatter.26.cloned.1.call-update) | async-done | bytes 36880
  1119.8 4.6 all-reduce.4
  1125.0 43.1 %all_gather.49 = f32[384,384]{0,1:T(8,128)S(1)} all-gather(f32[384,24]{0,1:T(8,128)S(1)} %get-tuple-element.133), channel_id=1, replica_groups=mesh['shard'=16,'ctx'=2] {'shard'}, dimensions={1}, use_global_device_ids=true | all-gather | bytes 626688 | tf_op jit(solution)/shard_map/all_gather | solution.py:287
  1238.7 7.4 all-gather.24.cloned.1.call-done
  1249.8 60.6 %all-gather.26.cloned.1.call-done = f32[384,1536]{0,1:T(8,128)} async-done(((f32[384,96]{0,1:T(8,128)}), f32[384,1536]{0,1:T(8,128)}) %all-gather.26.cloned.1.call-update) | async-done | bytes 2359312 | tf_op jit(solution)/shard_map/all_gather | solution.py:289
  1319.3 5.2 convolution_add_fusion.16
  1329.9 5.1 convolution_add_fusion.15
  1334.9 4.5 fusion.128
  1340.8 5.1 convolution_add_fusion.14
  1351.4 5.1 convolution_add_fusion.13
  1361.9 5.2 fusion.131
  1373.0 5.4 convolution_add_fusion.12
  1383.8 5.2 convolution_add_fusion.11
  1394.5 5.1 convolution_add_fusion.10
  1405.1 5.1 convolution_add_fusion.9
  1416.0 5.0 fusion.136
  1429.2 9.1 fusion.34
  1439.6 6.3 convolution_add_fusion.4
  1446.0 5.9 fusion.111
  1453.2 6.5 convolution_add_fusion.3
  1459.7 5.9 fusion.112
  1466.9 6.3 convolution_add_fusion.2
  1473.2 5.9 fusion.113
  1480.4 6.3 convolution_add_fusion.1
  1486.8 5.9 fusion.114
  1494.0 6.3 fusion.115
  (357 shorter events, 207.4 us)
Async XLA Ops:
  7.2 128.6 %copy-start.63 = (bf16[1,384]{1,0:T(2,128)(2,1)S(1)}, bf16[1,384]{1,0:T(2,128)(2,1)}, u32[]{:S(2)}) copy-start(bf16[1,384]{1,0:T(2,128)(2,1)} %param.16) | copy-start | bytes 2308
  7.2 128.6 %all-gather.10.cloned.1.call-start = ((), (), s32[]{:S(2)}) async-start(), calls=%async_computation.7 | async-start | bytes 1880064 | tf_op jit(solution)/shard_map/all_gather | solution.py:95
  8.9 173.9 %all-gather.14.cloned.1.call-start = ((), (), s32[]{:S(2)}) async-start(), calls=%async_computation.9 | async-start | bytes 2359296 | tf_op jit(solution)/shard_map/all_gather | solution.py:127
  8.9 130.0 %copy-start.5 = (bf16[1,1024,384]{2,1,0:T(8,128)(2,1)S(1)}, bf16[1,1024,384]{2,1,0:T(8,128)(2,1)}, u32[]{:S(2)}) copy-start(bf16[1,1024,384]{2,1,0:T(8,128)(2,1)} %param.15) | copy-start | bytes 2359300
  92.9 45.4 %copy-start.50 = (f32[1024]{0:T(1024)}, f32[1024]{0:T(1024)S(1)}, u32[]{:S(2)}) copy-start(f32[1024]{0:T(1024)S(1)} %broadcast_multiply_fusion.11) | copy-start | bytes 12292
  94.5 43.9 %copy-start.58 = (f32[1024]{0:T(1024)}, f32[1024]{0:T(1024)S(1)}, u32[]{:S(2)}) copy-start(f32[1024]{0:T(1024)S(1)} %add_rsqrt_fusion.1) | copy-start | bytes 12292
  138.3 110.4 %copy-start.78 = (f32[384]{0:T(512)}, f32[384]{0:T(512)S(1)}, u32[]{:S(2)}) copy-start(f32[384]{0:T(512)S(1)} %get-tuple-element.114) | copy-start | bytes 4612
  138.3 158.7 %copy-start.68 = (f32[384]{0:T(512)}, f32[384]{0:T(512)S(1)}, u32[]{:S(2)}) copy-start(f32[384]{0:T(512)S(1)} %get-tuple-element.115) | copy-start | bytes 4612
  138.3 158.7 %copy-start.70 = (f32[384]{0:T(512)}, f32[384]{0:T(512)S(1)}, u32[]{:S(2)}) copy-start(f32[384]{0:T(512)S(1)} %get-tuple-element.113) | copy-start | bytes 4612
  141.9 82.9 %all-gather.12.cloned.1.call-start = ((), (), s32[]{:S(2)}) async-start(), calls=%async_computation.8 | async-start | bytes 2359296 | tf_op jit(solution)/shard_map/all_gather | solution.py:128
  142.6 106.1 %all-gather.16.cloned.1.call-start = ((), (), s32[]{:S(2)}) async-start(), calls=%async_computation.10 | async-start | bytes 1253376 | tf_op jit(solution)/shard_map/all_gather | solution.py:98
  143.4 137.3 %all-gather.18.cloned.1.call-start = ((), (), s32[]{:S(2)}) async-start(), calls=%async_computation.11 | async-start | bytes 1253376 | tf_op jit(solution)/shard_map/all_gather | solution.py:99
  144.1 282.2 %reduce-scatter.16.cloned.1.call-start = ((), (), s32[]{:S(2)}) async-start(), calls=%async_computation.13 | async-start | bytes 4718592 | tf_op jit(solution)/shard_map/reduce_scatter | solution.py:204
  248.3 48.8 %copy-start.3 = (f32[1,1024,384]{2,1,0:T(8,128)}, f32[1,1024,384]{2,1,0:T(8,128)S(1)}, u32[]{:S(2)}) copy-start(f32[1,1024,384]{2,1,0:T(8,128)S(1)} %get-tuple-element.143) | copy-start | bytes 4718596
  248.3 48.8 %copy-start.53 = (f32[1024]{0:T(1024)}, f32[1024]{0:T(1024)S(1)}, u32[]{:S(2)}) copy-start(f32[1024]{0:T(1024)S(1)} %broadcast_multiply_fusion.10) | copy-start | bytes 12292
  248.7 48.4 %copy-start.61 = (f32[1024]{0:T(1024)}, f32[1024]{0:T(1024)S(1)}, u32[]{:S(2)}) copy-start(f32[1024]{0:T(1024)S(1)} %add_rsqrt_fusion) | copy-start | bytes 12292
  320.8 108.8 %reduce-scatter.14.cloned.1.call-start = ((), (), s32[]{:S(2)}) async-start(), calls=%async_computation.12 | async-start | bytes 4718592 | tf_op jit(solution)/shard_map/reduce_scatter | solution.py:201
  356.0 40.5 %copy-start.12 = (bf16[1,1024,384]{1,2,0:T(8,128)(2,1)S(1)}, bf16[1,1024,384]{1,2,0:T(8,128)(2,1)}, u32[]{:S(2)}) copy-start(bf16[1,1024,384]{1,2,0:T(8,128)(2,1)} %copy-done.11) | copy-start | bytes 2359300
  410.9 163.2 %reduce-scatter.22.cloned.1.call-start = ((), (), s32[]{:S(2)}) async-start(), calls=%async_computation.20 | async-start | bytes 3760128
  441.0 265.6 %reduce-scatter.20.cloned.1.call-start = ((), (), s32[]{:S(2)}) async-start(), calls=%async_computation.18 | async-start | bytes 2506752 | tf_op jit(solution)/shard_map/reduce_scatter | solution.py:253
  447.3 392.2 %reduce-scatter.18.cloned.1.call-start = ((), (), s32[]{:S(2)}) async-start(), calls=%async_computation.16 | async-start | bytes 2506752 | tf_op jit(solution)/shard_map/reduce_scatter | solution.py:252
  454.2 515.9 %reduce-scatter.24.cloned.1.call-start = ((), (), s32[]{:S(2)}) async-start(), calls=%async_computation.21 | async-start | bytes 1880064
  458.5 511.7 %copy-start.10 = (bf16[1024,384]{1,0:T(8,128)(2,1)S(1)}, bf16[1024,384]{1,0:T(8,128)(2,1)}, u32[]{:S(2)}) copy-start(bf16[1024,384]{1,0:T(8,128)(2,1)} %copy-done.9) | copy-start | bytes 2359300
  458.6 511.7 %copy-start.18 = (bf16[6,64,1024]{2,1,0:T(8,128)(2,1)S(1)}, bf16[6,64,1024]{2,1,0:T(8,128)(2,1)}, u32[]{:S(2)}) copy-start(bf16[6,64,1024]{2,1,0:T(8,128)(2,1)} %copy-done.17) | copy-start | bytes 2359300
  458.6 532.3 %copy-start.47 = (f32[384,72]{0,1:T(8,128)S(1)}, f32[384,72]{0,1:T(8,128)}, u32[]{:S(2)}) copy-start(f32[384,72]{0,1:T(8,128)} %param.25) | copy-start | bytes 331780
  458.6 532.3 %all-reduce.8.cloned.1.call-start = ((), (), s32[]{:S(2)}) async-start(), calls=%async_computation.23 | async-start | bytes 1597440 | tf_op jit(solution)/shard_map/psum | solution.py:256
  574.1 418.5 %copy-start.44 = (f32[384,96]{0,1:T(8,128)S(1)}, f32[384,96]{0,1:T(8,128)}, u32[]{:S(2)}) copy-start(f32[384,96]{0,1:T(8,128)} %param.27) | copy-start | bytes 442372
  970.2 25.0 %copy-start.26 = (f32[384,144]{0,1:T(8,128)S(1)}, f32[384,144]{0,1:T(8,128)}, u32[]{:S(2)}) copy-start(f32[384,144]{0,1:T(8,128)} %param.18) | copy-start | bytes 663556
  970.2 25.9 %copy-start.40 = (f32[384,144]{0,1:T(8,128)S(1)}, f32[384,144]{0,1:T(8,128)}, u32[]{:S(2)}) copy-start(f32[384,144]{0,1:T(8,128)} %param.24) | copy-start | bytes 663556
  970.2 149.6 %reduce-scatter.26.cloned.1.call-start = ((), (), s32[]{:S(2)}) async-start(), calls=%async_computation.22 | async-start | bytes 626688
  971.7 25.4 %copy-start.74 = (f32[384]{0:T(512)S(1)}, f32[384]{0:T(512)}, u32[]{:S(2)}) copy-start(f32[384]{0:T(512)} %get-tuple-element.140) | copy-start | bytes 4612
  971.7 25.4 %copy-start.67 = (f32[384]{0:T(512)S(1)}, f32[384]{0:T(512)}, u32[]{:S(2)}) copy-start(f32[384]{0:T(512)} %get-tuple-element.137) | copy-start | bytes 4612
  971.7 25.5 %copy-start.72 = (f32[1536]{0:T(1024)S(1)}, f32[1536]{0:T(1024)}, u32[]{:S(2)}) copy-start(f32[1536]{0:T(1024)} %get-tuple-element.171) | copy-start | bytes 18436
  971.7 25.5 %copy-start.66 = (f32[384]{0:T(512)S(1)}, f32[384]{0:T(512)}, u32[]{:S(2)}) copy-start(f32[384]{0:T(512)} %get-tuple-element.153) | copy-start | bytes 4612
  971.7 102.6 %copy-start.7 = (bf16[384,2304]{0,1:T(8,128)(2,1)S(1)}, bf16[384,2304]{0,1:T(8,128)(2,1)}, u32[]{:S(2)}) copy-start(bf16[384,2304]{0,1:T(8,128)(2,1)} %all-gather.10.cloned.1.call-done) | copy-start | bytes 5308420
  971.7 102.6 %copy-start.49 = (f32[1,2304]{1,0:T(1,128)S(1)}, f32[1,2304]{1,0:T(1,128)}, u32[]{:S(2)}) copy-start(f32[1,2304]{1,0:T(1,128)} %copy-done.48) | copy-start | bytes 27652
  971.7 102.6 %copy-start.65 = (bf16[1,384]{1,0:T(2,128)(2,1)S(1)}, bf16[1,384]{1,0:T(2,128)(2,1)}, u32[]{:S(2)}) copy-start(bf16[1,384]{1,0:T(2,128)(2,1)} %param.16) | copy-start | bytes 2308
  971.8 221.8 %all-gather.22.cloned.1.call-start = ((), (), s32[]{:S(2)}) async-start(), calls=%async_computation.15 | async-start | bytes 1880064 | tf_op jit(solution)/shard_map/all_gather | solution.py:286
  992.5 253.6 %all-gather.24.cloned.1.call-start = ((), (), s32[]{:S(2)}) async-start(), calls=%async_computation.17 | async-start | bytes 2506752 | tf_op jit(solution)/shard_map/all_gather | solution.py:288
  994.2 130.2 %copy-start.52 = (f32[384,24]{0,1:T(8,128)S(1)}, f32[384,24]{0,1:T(8,128)}, u32[]{:S(2)}) copy-start(f32[384,24]{0,1:T(8,128)} %param.26) | copy-start | bytes 110596
  994.2 316.2 %all-gather.26.cloned.1.call-start = ((), (), s32[]{:S(2)}) async-start(), calls=%async_computation.19 | async-start | bytes 2506752 | tf_op jit(solution)/shard_map/all_gather | solution.py:289
  1074.4 96.5 %copy-start.45 = (f32[384,96]{0,1:T(8,128)S(1)}, f32[384,96]{0,1:T(8,128)}, u32[]{:S(2)}) copy-start(f32[384,96]{0,1:T(8,128)} %param.28) | copy-start | bytes 442372
  1074.4 96.5 %copy-start.46 = (f32[384,96]{0,1:T(8,128)S(1)}, f32[384,96]{0,1:T(8,128)}, u32[]{:S(2)}) copy-start(f32[384,96]{0,1:T(8,128)} %get-tuple-element.125) | copy-start | bytes 442372
  1075.2 96.8 %copy-start.73 = (f32[336]{0:T(512)S(1)}, f32[336]{0:T(512)}, u32[]{:S(2)}) copy-start(f32[336]{0:T(512)} %param.23) | copy-start | bytes 4036
  1075.2 96.8 %copy-start.75 = (f32[336]{0:T(512)S(1)}, f32[336]{0:T(512)}, u32[]{:S(2)}) copy-start(f32[336]{0:T(512)} %param.29) | copy-start | bytes 4036
  1125.0 44.5 %copy-start.41 = (f32[384,24]{0,1:T(8,128)}, f32[384,24]{0,1:T(8,128)S(1)}, u32[]{:S(2)}) copy-start(f32[384,24]{0,1:T(8,128)S(1)} %get-tuple-element.133) | copy-start | bytes 110596
  1171.7 250.0 %all-gather.20.cloned.1.call-start = ((), (), s32[]{:S(2)}) async-start(), calls=%async_computation.14 | async-start | bytes 3760128 | tf_op jit(solution)/shard_map/all_gather | solution.py:285
  1246.1 67.9 %copy-start.21 = (f32[384,1536]{0,1:T(8,128)S(1)}, f32[384,1536]{0,1:T(8,128)}, u32[]{:S(2)}) copy-start(f32[384,1536]{0,1:T(8,128)} %all-gather.24.cloned.1.call-done) | copy-start | bytes 7077892
  (53 other events, 239.0 us)
Sparse Core Ops, SparseCore 0:
  11.4 61.9 all-gather.9
  142.0 6.5 all-gather.13
  150.8 10.9 all-gather.11
  165.0 57.2 all-gather.15
  225.6 55.0 all-gather.17
  321.0 9.7 reduce-scatter.15
  411.0 9.4 reduce-scatter.13
  441.2 132.9 reduce-scatter.21
  579.0 127.5 reduce-scatter.19
  712.1 127.3 reduce-scatter.17
  844.4 125.7 reduce-scatter.23
  972.6 18.2 all-reduce.7
  996.3 123.4 reduce-scatter.25
  1123.0 58.7 all-gather.21
  1185.0 61.0 all-gather.23
  1249.3 61.0 all-gather.25
  1313.7 70.0 all-gather.19
where the time goes:
time: 1510 us
  waiting for transfers between devices  667 us (44%)
  matrix products  404 us (27%)
  blocking collectives  283 us (19%)
  other arithmetic  101 us (7%)
  local copies, waits for them, and re-layouts  31.4 us (2%)
  between operations  20.7 us (1%)
    unnamed x20, waiting for transfers between devices  292 us
    unnamed x2, blocking collectives  156 us
    reduce_scatter x1, waiting for transfers between devices, on_device(): lax.psum_scatter(expand_grad, 'shard', scatter_dimension=1, tiled=True)  133 us
    reduce_scatter x1, waiting for transfers between devices, on_device(): lax.psum_scatter(reduce_grad, 'shard', scatter_dimension=1, tiled=True)  131 us
    dot_general x25, matrix products, newton_whole(): jnp.dot(polynomial, iterate, precision=precise)  106 us
    dot_general x25, matrix products, newton_whole(): gram_now = jnp.dot(iterate, iterate.T, precision=precise)  97.5 us
    all_gather x1, waiting for transfers between devices, on_device(): lax.all_gather(matrices[4], 'shard', axis=1, tiled=True)  60.6 us
    all_gather x1, blocking collectives, on_device(): lax.all_gather(matrices[2], 'shard', axis=1, tiled=True)  43.1 us
  transfers between devices with their start and end apart: 17, of which 9 were waited for; matrix products, arithmetic and copies ran while one was open for 26% of the time, Pallas kernels for 0%

commit v1 on v0

--- a/solution.py
+++ b/solution.py
@@ -18,6 +18,24 @@
 matrix_rate = 0.5
 bias_rate = 0.1
 precise = lax.Precision.HIGHEST
+
+
+def ring_gather(array, axis, dim):
+    ways, here, step = (lax.axis_size(axis), lax.axis_index(axis), array.shape[dim])
+    dims = [n * ways if d == dim else n for d, n in enumerate(array.shape)]
+    full = lax.dynamic_update_slice_in_dim(
+        jnp.zeros(dims, array.dtype), array, here * step, axis=dim
+    )
+    going_up = going_down = array
+    for far in range(1, ways // 2 + 1):
+        going_up = lax.ppermute(going_up, axis, [(d, (d + 1) % ways) for d in range(ways)])
+        full = lax.dynamic_update_slice_in_dim(full, going_up, (here - far) % ways * step, axis=dim)
+        if 2 * far < ways:
+            going_down = lax.ppermute(going_down, axis, [(d, (d - 1) % ways) for d in range(ways)])
+            full = lax.dynamic_update_slice_in_dim(
+                full, going_down, (here + far) % ways * step, axis=dim
+            )
+    return full
 
 
 def silu_of(values):
@@ -286,7 +304,7 @@
         lax.all_gather(matrices[1], "shard", axis=1, tiled=True),
         lax.all_gather(matrices[2], "shard", axis=1, tiled=True),
         lax.all_gather(matrices[3], "shard", axis=1, tiled=True),
-        lax.all_gather(matrices[4], "shard", axis=1, tiled=True),
+        ring_gather(matrices[4], "shard", 1),
     )
     position = lax.axis_index("shard")
     directions = tuple(

time: 1510 us -> 1520 us (level)
  starting transfers between devices: 0.91 us -> 36.3 us
  waiting for transfers between devices: 667 us -> 642 us
    all_gather x1 -> x0, waiting for transfers between devices: 60.6 us -> none  [on_device(): lax.all_gather(matrices[4], 'shard', axis=1, tiled=True)]
    ppermute x0 -> x15, waiting for transfers between devices: none -> 41.2 us  [the longest x7 22.3 us: ring_gather(): lax.ppermute(going_down, axis, [(d, (d - 1) % ways) for d in range(ways)])]
    ppermute x0 -> x15, starting transfers between devices: none -> 35.5 us  [the longest x7 32.9 us: ring_gather(): lax.ppermute(going_down, axis, [(d, (d - 1) % ways) for d in range(ways)])]
    unnamed x20 -> x19, waiting for transfers between devices: 292 us -> 293 us
  transfers between devices with their start and end apart: 17 -> 31, of which waited for: 9 -> 17; matrix products, arithmetic and copies ran while one was open for 26% -> 26% of each run, Pallas kernels for 0% -> 0%
where the time goes in v1:
time: 1520 us
  waiting for transfers between devices  642 us (42%)
  matrix products  404 us (27%)
  blocking collectives  283 us (19%)
  other arithmetic  99.1 us (7%)
  starting transfers between devices  36.3 us (2%)
  local copies, waits for them, and re-layouts  33.3 us (2%)
  between operations  21.1 us (1%)
    unnamed x19, waiting for transfers between devices  293 us
    unnamed x2, blocking collectives  156 us
    reduce_scatter x1, waiting for transfers between devices, on_device(): lax.psum_scatter(expand_grad, 'shard', scatter_dimension=1, tiled=True)  133 us
    reduce_scatter x1, waiting for transfers between devices, on_device(): lax.psum_scatter(reduce_grad, 'shard', scatter_dimension=1, tiled=True)  131 us
    dot_general x25, matrix products, newton_whole(): jnp.dot(polynomial, iterate, precision=precise)  106 us
    dot_general x25, matrix products, newton_whole(): gram_now = jnp.dot(iterate, iterate.T, precision=precise)  97.3 us
    all_gather x1, blocking collectives, on_device(): lax.all_gather(matrices[2], 'shard', axis=1, tiled=True)  43.1 us
    all_gather x1, blocking collectives, on_device(): lax.all_gather(attend_weight.astype(bfloat), 'shard', axis=1, tiled=True)  41.3 us
  transfers between devices with their start and end apart: 31, of which 17 were waited for; matrix products, arithmetic and copies ran while one was open for 26% of the time, Pallas kernels for 0%

profile of v1, /device:TPU:0, one launch (start us, length us, event | category | flops | bytes accessed | tf_op | source)
XLA Modules:
  0.0 1518.9 jit_solution(1889626900272511548)
XLA Ops:
  11.9 78.7 %all-reduce = bf16[5376]{0:T(1024)(128)(2,1)S(1)} all-reduce(bf16[5376]{0:T(1024)(128)(2,1)S(1)} %dynamic-update-slice), channel_id=1, replica_groups=mesh['shard'=16,'ctx'=2] {'shard'}, use_global_device_ids=true, to_apply=%add | all-reduce | flops 5376 | bytes 21504
  94.5 41.3 %all_gather.38 = bf16[384,1152]{0,1:T(8,128)(2,1)S(1)} all-gather(bf16[384,72]{0,1:T(8,128)(2,1)S(1)} %convert_element_type.109), channel_id=1, replica_groups=mesh['shard'=16,'ctx'=2] {'shard'}, dimensions={1}, use_global_device_ids=true | all-gather | bytes 940032 | tf_op jit(solution)/shard_map/all_gather | solution.py:114
  144.2 38.5 %all_gather.41 = bf16[384,384]{0,1:T(8,128)(2,1)S(1)} all-gather(bf16[384,24]{0,1:T(8,128)(2,1)S(1)} %convert_element_type.115), channel_id=1, replica_groups=mesh['shard'=16,'ctx'=2] {'shard'}, dimensions={1}, use_global_device_ids=true | all-gather | bytes 313344 | tf_op jit(solution)/shard_map/all_gather | solution.py:115
  185.0 19.5 %multiply_reduce_fusion.1 = (f32[6,1024]{1,0:T(8,128)S(1)}, f32[6,1024,2048]{2,1,0:T(8,128)}) fusion(bf16[1024,6,64]{0,2,1:T(8,128)(2,1)S(1)} %bitcast.262, bf16[2048,6,64]{0,2,1:T(8,128)(2,1)S(1)} %bitcast.257), kind=kOutput, calls=%fused_computation.6 | convolution fusion | flops 1635772416 | bytes 52715520 | tf_op jit(solution)/shard_map/lqhd,lkhd->lhqk/dot_general | solution.py:153
  204.5 20.5 %fusion = f32[6,1024]{1,0:T(8,128)S(1)} fusion(f32[6,1024,2048]{2,1,0:T(8,128)} %get-tuple-element.164, f32[6,1024]{1,0:T(8,128)S(1)} %get-tuple-element.163), kind=kLoop, calls=%fused_computation.5 | loop fusion | flops 37742592 | bytes 50380800 | tf_op jit(solution)/shard_map/reduce_sum | solution.py:158
  226.7 19.8 %fusion.35 = bf16[6,64,1024]{2,1,0:T(8,128)(2,1)S(1)} fusion(bf16[2048,6,64]{0,2,1:T(8,128)(2,1)S(1)} %bitcast.266, f32[6,1024,2048]{2,1,0:T(8,128)} %get-tuple-element.164, f32[6,1024]{1,0:T(8,128)S(1)} %fusion, f32[6,1024]{1,0:T(8,128)S(1)} %get-tuple-element.163), kind=kOutput, calls=%fused_computation.93 | convolution fusion | flops 1661337600 | bytes 52740096 | tf_op jit(solution)/shard_map/lhqk,lkhd->lqhd/dot_general | solution.py:162
  248.9 6.9 multiply_convert_fusion.1
  255.9 24.8 %all-gather.17.cloned.1.call-done = bf16[384,1536]{0,1:T(8,128)(2,1)} async-done(((bf16[384,96]{0,1:T(8,128)(2,1)}), bf16[384,1536]{0,1:T(8,128)(2,1)}) %all-gather.17.cloned.1.call-update) | async-done | bytes 1179664 | tf_op jit(solution)/shard_map/all_gather | solution.py:117
  280.7 9.9 convert_reduce_fusion
  301.5 19.6 %fusion.2 = f32[6,64,2048]{2,1,0:T(8,128)} fusion(bf16[1024,6,64]{0,2,1:T(8,128)(2,1)S(1)} %bitcast.264, f32[6,1024,2048]{2,1,0:T(8,128)} %get-tuple-element.164, f32[6,1024]{1,0:T(8,128)S(1)} %log_add_fusion), kind=kOutput, calls=%fused_computation.8 | convolution fusion | flops 1648361472 | bytes 54288384 | tf_op jit(solution)/shard_map/lhqk,lqhd->lkhd/dot_general | solution.py:203
  321.1 34.9 %multiply_reduce_fusion = (f32[6,1024]{1,0:T(8,128)S(1)}, f32[6,1024,2048]{2,1,0:T(8,128)}) fusion(f32[6,1024,2048]{2,1,0:T(8,128)} %get-tuple-element.164, f32[6,1024]{1,0:T(8,128)S(1)} %log_add_fusion, bf16[1024,6,64]{0,2,1:T(8,128)(2,1)S(1)} %bitcast.265, bf16[2048,6,64]{0,2,1:T(8,128)(2,1)} %bitcast.267), kind=kOutput, calls=%fused_computation.1 | convolution fusion | flops 1660938240 | bytes 103071744 | tf_op jit(solution)/shard_map/lqhd,lkhd->lhqk/dot_general | solution.py:200
  356.0 40.5 %multiply_convert_fusion = bf16[6,1024,2048]{2,1,0:T(8,128)(2,1)} fusion(f32[6,1024,2048]{2,1,0:T(8,128)} %get-tuple-element.170, f32[6,1024,2048]{2,1,0:T(8,128)} %get-tuple-element.164, f32[6,1024]{1,0:T(8,128)S(1)} %get-tuple-element.169, f32[6,1024]{1,0:T(8,128)S(1)} %log_add_fusion), kind=kLoop, calls=%fused_computation | loop fusion | flops 62914560 | bytes 125878272 | tf_op jit(solution)/shard_map/convert_element_type | solution.py:208
  396.5 14.3 convolution_multiply_fusion
  412.2 14.2 multiply_convert_fusion.2
  442.2 5.1 fusion.68
  448.8 5.5 fusion.113
  458.8 115.3 %reduce-scatter.22.cloned.1.call-done = f32[144,384]{1,0:T(8,128)} async-done(((f32[2304,384]{1,0:T(8,128)}), f32[144,384]{1,0:T(8,128)}) %reduce-scatter.22.cloned.1.call-update) | async-done | bytes 221200
  575.9 130.8 %reduce-scatter.20.cloned.1.call-done = f32[384,96]{0,1:T(8,128)} async-done(((f32[384,1536]{0,1:T(8,128)}), f32[384,96]{0,1:T(8,128)}) %reduce-scatter.20.cloned.1.call-update) | async-done | bytes 147472 | tf_op jit(solution)/shard_map/reduce_scatter | solution.py:271
  706.7 133.2 %reduce-scatter.18.cloned.1.call-done = f32[384,96]{0,1:T(8,128)} async-done(((f32[384,1536]{0,1:T(8,128)}), f32[384,96]{0,1:T(8,128)}) %reduce-scatter.18.cloned.1.call-update) | async-done | bytes 147472 | tf_op jit(solution)/shard_map/reduce_scatter | solution.py:270
  839.9 130.6 %reduce-scatter.24.cloned.1.call-done = f32[384,72]{0,1:T(8,128)} async-done(((f32[384,1152]{0,1:T(8,128)}), f32[384,72]{0,1:T(8,128)}) %reduce-scatter.24.cloned.1.call-update) | async-done | bytes 110608
  972.4 18.8 %all-reduce.8.cloned.1.call-done = (f32[384,144]{1,0:T(8,128)}, f32[384,72]{0,1:T(8,128)}, f32[384,96]{0,1:T(8,128)}, f32[384,96]{0,1:T(8,128)}) async-done(((f32[384,144]{1,0:T(8,128)}, f32[384,72]{0,1:T(8,128)}, f32[384,96]{0,1:T(8,128)}, f32[384,96]{0,1:T(8,128)}), (f32[384,144]{1,0:T(8,128)}, f32[384,72]{0,1:T(8,128)}, f32[384,96]{0,1:T(8,128)}, f32[384,96]{0,1:T(8,128)})) %all-reduce.8.cloned.1.call-update) | async-done | bytes 626704 | tf_op jit(solution)/shard_map/psum | solution.py:274
  996.2 77.1 %all-reduce.3 = f32[5376]{0:T(1024)S(1)} all-reduce(f32[5376]{0:T(1024)S(1)} %constant_dynamic-update-slice_fusion.23), channel_id=9, replica_groups=mesh['shard'=16,'ctx'=2] {'shard'}, use_global_device_ids=true, to_apply=%region_40.41.clone | all-reduce | flops 5376 | bytes 43008
  1074.1 46.0 %reduce-scatter.26.cloned.1.call-done = f32[384,24]{0,1:T(8,128)} async-done(((f32[384,384]{0,1:T(8,128)}), f32[384,24]{0,1:T(8,128)}) %reduce-scatter.26.cloned.1.call-update) | async-done | bytes 36880
  1125.4 43.1 %all_gather.46 = f32[384,384]{0,1:T(8,128)S(1)} all-gather(f32[384,24]{0,1:T(8,128)S(1)} %get-tuple-element.134), channel_id=1, replica_groups=mesh['shard'=16,'ctx'=2] {'shard'}, dimensions={1}, use_global_device_ids=true | all-gather | bytes 626688 | tf_op jit(solution)/shard_map/all_gather | solution.py:305
  1207.2 6.1 collective-permute-start.5
  1213.9 5.9 collective-permute-done.5
  1219.8 6.1 collective-permute-start.7
  1229.2 6.1 collective-permute-start.9
  1235.3 5.5 collective-permute-done.9
  1240.8 6.1 collective-permute-start.11
  1250.7 6.0 collective-permute-start.13
  1256.7 8.7 collective-permute-done.12
  1265.7 8.7 collective-permute-done.14
  1302.8 5.1 convolution_add_fusion.10
  1313.5 5.1 convolution_add_fusion.9
  1324.0 5.4 fusion.148
  1384.1 5.1 convolution_add_fusion.14
  1426.6 5.2 fusion.144
  1439.8 9.1 fusion.34
  1450.3 6.5 convolution_add_fusion.4
  1456.8 5.9 fusion.124
  1464.0 6.3 convolution_add_fusion.3
  1470.3 5.9 fusion.125
  1477.5 6.3 convolution_add_fusion.2
  1483.9 5.9 fusion.126
  1491.1 6.5 convolution_add_fusion.1
  1497.6 5.9 fusion.127
  1504.8 6.2 fusion.128
  (402 shorter events, 259.1 us)
Async XLA Ops:
  7.2 128.6 %copy-start.64 = (bf16[1,384]{1,0:T(2,128)(2,1)S(1)}, bf16[1,384]{1,0:T(2,128)(2,1)}, u32[]{:S(2)}) copy-start(bf16[1,384]{1,0:T(2,128)(2,1)} %param.16) | copy-start | bytes 2308
  7.2 128.6 %all-gather.9.cloned.1.call-start = ((), (), s32[]{:S(2)}) async-start(), calls=%async_computation.7 | async-start | bytes 1880064 | tf_op jit(solution)/shard_map/all_gather | solution.py:113
  8.9 174.1 %all-gather.13.cloned.1.call-start = ((), (), s32[]{:S(2)}) async-start(), calls=%async_computation.9 | async-start | bytes 2359296 | tf_op jit(solution)/shard_map/all_gather | solution.py:145
  8.9 129.9 %copy-start.5 = (bf16[1,1024,384]{2,1,0:T(8,128)(2,1)S(1)}, bf16[1,1024,384]{2,1,0:T(8,128)(2,1)}, u32[]{:S(2)}) copy-start(bf16[1,1024,384]{2,1,0:T(8,128)(2,1)} %param.15) | copy-start | bytes 2359300
  92.9 45.4 %copy-start.51 = (f32[1024]{0:T(1024)}, f32[1024]{0:T(1024)S(1)}, u32[]{:S(2)}) copy-start(f32[1024]{0:T(1024)S(1)} %broadcast_multiply_fusion.11) | copy-start | bytes 12292
  138.3 110.6 %copy-start.79 = (f32[384]{0:T(512)}, f32[384]{0:T(512)S(1)}, u32[]{:S(2)}) copy-start(f32[384]{0:T(512)S(1)} %get-tuple-element.114) | copy-start | bytes 4612
  138.3 159.0 %copy-start.69 = (f32[384]{0:T(512)}, f32[384]{0:T(512)S(1)}, u32[]{:S(2)}) copy-start(f32[384]{0:T(512)S(1)} %get-tuple-element.115) | copy-start | bytes 4612
  138.3 158.9 %copy-start.71 = (f32[384]{0:T(512)}, f32[384]{0:T(512)S(1)}, u32[]{:S(2)}) copy-start(f32[384]{0:T(512)S(1)} %get-tuple-element.113) | copy-start | bytes 4612
  141.9 83.1 %all-gather.11.cloned.1.call-start = ((), (), s32[]{:S(2)}) async-start(), calls=%async_computation.8 | async-start | bytes 2359296 | tf_op jit(solution)/shard_map/all_gather | solution.py:146
  142.6 106.3 %all-gather.15.cloned.1.call-start = ((), (), s32[]{:S(2)}) async-start(), calls=%async_computation.10 | async-start | bytes 1253376 | tf_op jit(solution)/shard_map/all_gather | solution.py:116
  143.4 137.3 %all-gather.17.cloned.1.call-start = ((), (), s32[]{:S(2)}) async-start(), calls=%async_computation.11 | async-start | bytes 1253376 | tf_op jit(solution)/shard_map/all_gather | solution.py:117
  144.1 282.4 %reduce-scatter.16.cloned.1.call-start = ((), (), s32[]{:S(2)}) async-start(), calls=%async_computation.13 | async-start | bytes 4718592 | tf_op jit(solution)/shard_map/reduce_scatter | solution.py:222
  248.5 48.8 %copy-start.3 = (f32[1,1024,384]{2,1,0:T(8,128)}, f32[1,1024,384]{2,1,0:T(8,128)S(1)}, u32[]{:S(2)}) copy-start(f32[1,1024,384]{2,1,0:T(8,128)S(1)} %get-tuple-element.144) | copy-start | bytes 4718596
  248.5 48.8 %copy-start.54 = (f32[1024]{0:T(1024)}, f32[1024]{0:T(1024)S(1)}, u32[]{:S(2)}) copy-start(f32[1024]{0:T(1024)S(1)} %broadcast_multiply_fusion.10) | copy-start | bytes 12292
  248.9 48.4 %copy-start.62 = (f32[1024]{0:T(1024)}, f32[1024]{0:T(1024)S(1)}, u32[]{:S(2)}) copy-start(f32[1024]{0:T(1024)S(1)} %add_rsqrt_fusion) | copy-start | bytes 12292
  321.1 108.6 %reduce-scatter.14.cloned.1.call-start = ((), (), s32[]{:S(2)}) async-start(), calls=%async_computation.12 | async-start | bytes 4718592 | tf_op jit(solution)/shard_map/reduce_scatter | solution.py:219
  410.8 163.2 %reduce-scatter.22.cloned.1.call-start = ((), (), s32[]{:S(2)}) async-start(), calls=%async_computation.19 | async-start | bytes 3760128
  441.1 265.6 %reduce-scatter.20.cloned.1.call-start = ((), (), s32[]{:S(2)}) async-start(), calls=%async_computation.18 | async-start | bytes 2506752 | tf_op jit(solution)/shard_map/reduce_scatter | solution.py:271
  447.4 392.5 %reduce-scatter.18.cloned.1.call-start = ((), (), s32[]{:S(2)}) async-start(), calls=%async_computation.16 | async-start | bytes 2506752 | tf_op jit(solution)/shard_map/reduce_scatter | solution.py:270
  454.3 516.2 %reduce-scatter.24.cloned.1.call-start = ((), (), s32[]{:S(2)}) async-start(), calls=%async_computation.20 | async-start | bytes 1880064
  458.7 512.2 %copy-start.10 = (bf16[1024,384]{1,0:T(8,128)(2,1)S(1)}, bf16[1024,384]{1,0:T(8,128)(2,1)}, u32[]{:S(2)}) copy-start(bf16[1024,384]{1,0:T(8,128)(2,1)} %copy-done.9) | copy-start | bytes 2359300
  458.7 512.2 %copy-start.18 = (bf16[6,64,1024]{2,1,0:T(8,128)(2,1)S(1)}, bf16[6,64,1024]{2,1,0:T(8,128)(2,1)}, u32[]{:S(2)}) copy-start(bf16[6,64,1024]{2,1,0:T(8,128)(2,1)} %copy-done.17) | copy-start | bytes 2359300
  458.7 532.5 %copy-start.48 = (f32[384,72]{0,1:T(8,128)S(1)}, f32[384,72]{0,1:T(8,128)}, u32[]{:S(2)}) copy-start(f32[384,72]{0,1:T(8,128)} %param.25) | copy-start | bytes 331780
  458.7 532.5 %all-reduce.8.cloned.1.call-start = ((), (), s32[]{:S(2)}) async-start(), calls=%async_computation.22 | async-start | bytes 1597440 | tf_op jit(solution)/shard_map/psum | solution.py:274
  575.9 417.3 %copy-start.37 = (f32[384,72]{0,1:T(8,128)S(1)}, f32[384,72]{0,1:T(8,128)}, u32[]{:S(2)}) copy-start(f32[384,72]{0,1:T(8,128)} %param.19) | copy-start | bytes 331780
  970.6 149.6 %reduce-scatter.26.cloned.1.call-start = ((), (), s32[]{:S(2)}) async-start(), calls=%async_computation.21 | async-start | bytes 626688
  972.3 101.0 %copy-start.7 = (bf16[384,2304]{0,1:T(8,128)(2,1)S(1)}, bf16[384,2304]{0,1:T(8,128)(2,1)}, u32[]{:S(2)}) copy-start(bf16[384,2304]{0,1:T(8,128)(2,1)} %all-gather.9.cloned.1.call-done) | copy-start | bytes 5308420
  972.3 101.0 %copy-start.50 = (f32[1,2304]{1,0:T(1,128)S(1)}, f32[1,2304]{1,0:T(1,128)}, u32[]{:S(2)}) copy-start(f32[1,2304]{1,0:T(1,128)} %copy-done.49) | copy-start | bytes 27652
  972.3 101.0 %copy-start.66 = (bf16[1,384]{1,0:T(2,128)(2,1)S(1)}, bf16[1,384]{1,0:T(2,128)(2,1)}, u32[]{:S(2)}) copy-start(bf16[1,384]{1,0:T(2,128)(2,1)} %param.16) | copy-start | bytes 2308
  972.3 357.8 %all-gather.21.cloned.1.call-start = ((), (), s32[]{:S(2)}) async-start(), calls=%async_computation.15 | async-start | bytes 1880064 | tf_op jit(solution)/shard_map/all_gather | solution.py:304
  992.8 382.2 %all-gather.23.cloned.1.call-start = ((), (), s32[]{:S(2)}) async-start(), calls=%async_computation.17 | async-start | bytes 2506752 | tf_op jit(solution)/shard_map/all_gather | solution.py:306
  992.9 131.8 %copy-start.53 = (f32[384,24]{0,1:T(8,128)S(1)}, f32[384,24]{0,1:T(8,128)}, u32[]{:S(2)}) copy-start(f32[384,24]{0,1:T(8,128)} %param.26) | copy-start | bytes 110596
  1173.4 259.1 %all-gather.19.cloned.1.call-start = ((), (), s32[]{:S(2)}) async-start(), calls=%async_computation.14 | async-start | bytes 3760128 | tf_op jit(solution)/shard_map/all_gather | solution.py:303
  1192.9 7.5 collective-permute-start.1
  1192.9 10.8 collective-permute-start
  1200.4 6.8 collective-permute-start.3
  1203.7 10.1 collective-permute-start.2
  1207.2 12.6 collective-permute-start.5
  1213.9 12.1 collective-permute-start.4
  1219.8 9.3 collective-permute-start.7
  1225.9 9.4 collective-permute-start.6
  1229.2 11.7 collective-permute-start.9
  1235.3 11.7 collective-permute-start.8
  1240.8 9.8 collective-permute-start.11
  1246.9 9.8 collective-permute-start.10
  1250.7 15.0 collective-permute-start.13
  1256.7 8.7 collective-permute-start.12
  1265.4 8.9 collective-permute-start.14
  (68 other events, 538.6 us)
Sparse Core Ops, SparseCore 0:
  11.4 61.9 all-gather.8
  142.0 6.6 all-gather.12
  150.8 10.9 all-gather.10
  165.1 57.2 all-gather.14
  225.6 55.0 all-gather.16
  321.2 9.7 reduce-scatter.15
  410.9 9.4 reduce-scatter.13
  441.2 132.7 reduce-scatter.21
  579.0 127.6 reduce-scatter.19
  712.2 127.6 reduce-scatter.17
  844.8 125.7 reduce-scatter.23
  973.0 18.1 all-reduce.7
  996.6 123.5 reduce-scatter.25
  1123.4 59.2 all-gather.20
  1185.9 71.9 all-gather.22
  1261.1 74.8 all-gather.18
